TPU v7x, 256 devices: a whole 4x4x8 slice. The times are simulated.
256 devices in a mesh: stn: 128 (over x, y_hi, z, core), blk: 2 (over y_lo).
Axes of the slice: x: 4, y: 4 (y_hi: 2, y_lo: 2; y = y_hi * 2 + y_lo), z: 8, core: 2. Of those that a mesh axis runs over, the one named last changes fastest.
Arguments:
- voltages: bfloat16 [1024, 2, 63, 2, 4096], P('stn', 'blk'), may hold values from -6 to 6
- station_map: int32 [512], replicated, may hold values from 0 to 511, each once
- chan_counts: int32 [128], replicated, may hold values from 1 to 3, 256 in all
Outputs:
- visibilities: bfloat16 [128, 3, 2, 1024, 1024], P('stn', None, None, 'blk')
Inputs may be any that keep to these rules, and one draw needn't show every extreme that they name: A permutation: stream rows 2 q and 2 q + 1 of voltages are the two polarizations of station station_map[q]. `chan_counts`: the counts sum to 256; the largest is 3; device d of stn correlates the consecutive channels that start at the sum of the counts before it.
All inputs are finite; a program needn't handle non-finite values.
Results may differ from a plain program's by a relative error of at most 0.0056.
Values may be sent and summed in bfloat16 or wider, within the bound.
A program may use at most 192 MiB of HBM per device.

v0:
```python
import math

import jax
import jax.numpy as jnp
from jax import lax
from jax.sharding import PartitionSpec as P

FFT_LEN = 4096
TAPS = 16
CAP = 3
NSPEC = 48


def prototype(tap_count, frame_len):
    span_len = tap_count * frame_len
    points = jnp.arange(span_len, dtype=jnp.float32) + 0.5
    window = 0.5 - 0.5 * jnp.cos(2.0 * math.pi * points / span_len)
    shifted = math.pi * (points - span_len / 2.0) / frame_len
    filt_vals = jnp.sin(shifted) / shifted * window
    filt_vals = filt_vals / jnp.sqrt(jnp.sum(filt_vals * filt_vals))
    return filt_vals.reshape(tap_count, frame_len)


def direct_dft(folded, band_len):
    frame_len = folded.shape[-1]
    positions = jnp.arange(frame_len, dtype=jnp.int32)
    channels = jnp.arange(band_len, dtype=jnp.int32)
    phase = (positions[:, None] * channels[None, :] % frame_len).astype(jnp.float32) * (
        2.0 * math.pi / frame_len
    )
    cosine = jnp.cos(phase)
    sine = jnp.sin(phase)
    table = jnp.concatenate(
        [jnp.concatenate([cosine, -sine], axis=1), jnp.concatenate([sine, cosine], axis=1)], axis=0
    )
    rows_in = folded.reshape(-1, 2 * frame_len)
    result = jnp.dot(
        rows_in, table, precision=lax.Precision.HIGHEST, preferred_element_type=jnp.float32
    )
    return result.reshape(folded.shape[:-2] + (2, band_len))


def body(voltages, station_map, chan_counts):
    stn_count = lax.axis_size("stn")
    band_len = 2 * stn_count
    signal = voltages[:, 0]
    local_rows = signal.shape[0]
    taper_table = prototype(TAPS, FFT_LEN)
    folded = jnp.zeros((local_rows, NSPEC, 2, FFT_LEN), jnp.float32)
    for tap_idx in range(TAPS):
        folded = (
            folded + signal[:, tap_idx : tap_idx + NSPEC].astype(jnp.float32) * taper_table[tap_idx]
        )
    spectra = direct_dft(folded, band_len)
    spectra = spectra.astype(jnp.bfloat16)
    offsets = jnp.cumsum(chan_counts) - chan_counts
    slot_range = jnp.arange(CAP, dtype=jnp.int32)
    pick_index = (
        offsets[:, None] + jnp.minimum(slot_range[None, :], chan_counts[:, None] - 1)
    ).reshape(-1)
    outgoing = jnp.take(spectra, pick_index, axis=3).reshape(local_rows, NSPEC, 2, stn_count, CAP)
    outgoing = outgoing.transpose(3, 4, 2, 0, 1)
    time_len = outgoing.shape[4]
    incoming = lax.all_to_all(
        outgoing.reshape(stn_count, -1), "stn", split_axis=0, concat_axis=0, tiled=True
    )
    incoming = incoming.reshape(stn_count, CAP, 2, local_rows, time_len).transpose(1, 2, 0, 3, 4)
    incoming = incoming.reshape(CAP, 2, stn_count * local_rows, time_len)
    incoming = lax.all_gather(incoming, "blk", axis=3, tiled=True)
    row_count = stn_count * local_rows
    station_total = row_count // 2
    inverse = (
        jnp.zeros((station_total,), jnp.int32)
        .at[station_map]
        .set(jnp.arange(station_total, dtype=jnp.int32))
    )
    true_rows = (2 * inverse[:, None] + jnp.arange(2, dtype=jnp.int32)[None, :]).reshape(-1)
    ordered = jnp.take(incoming, true_rows, axis=2)
    joined = jnp.concatenate([ordered[:, 0], ordered[:, 1]], axis=2)
    turned = jnp.concatenate([ordered[:, 1], -ordered[:, 0]], axis=2)
    groups = lax.axis_size("blk")
    half_rows = row_count // groups
    my_index = lax.axis_index("stn")
    live_count = chan_counts[my_index]
    valid_mask = (slot_range < live_count).astype(jnp.float32)[:, None, None, None]
    samples = ordered.shape[3]
    row_start = lax.axis_index("blk") * half_rows
    near_rows = lax.dynamic_slice_in_dim(joined, row_start, half_rows, 1)
    turn_rows = lax.dynamic_slice_in_dim(turned, row_start, half_rows, 1)
    stacked = jnp.concatenate([near_rows, turn_rows], axis=1)
    visibility = jnp.einsum("kit,kjt->kij", stacked, joined, preferred_element_type=jnp.float32)
    visibility = visibility.reshape(CAP, 2, half_rows, row_count) * (valid_mask / samples)
    return visibility.astype(jnp.bfloat16)[None]


def solution(mesh):
    return jax.shard_map(
        body,
        mesh=mesh,
        in_specs=(P("stn", "blk", None, None, None), P(), P()),
        out_specs=P("stn", None, None, "blk", None),
        check_vma=False,
    )
```

profile of v0, /device:TPU:1, one launch (start us, length us, event | category | flops | bytes accessed | tf_op | source)
XLA Modules:
  0.0 294.3 jit_solution(2143614473536556594)
XLA Ops:
  6.5 2.5 multiply_reduce_fusion
  9.0 17.6 %fusion.8 = (f32[4096,256]{0,1:T(8,128)}, f32[4096,256]{0,1:T(8,128)}) fusion(), kind=kLoop, calls=%fused_computation.18 | loop fusion | flops 14680064 | bytes 8388608 | tf_op jit(solution)/shard_map/sin | solution.py:32
  26.6 16.8 %fusion.10 = f32[4096,256]{0,1:T(8,128)} fusion(), kind=kLoop, calls=%fused_computation.20 | loop fusion | flops 15728640 | bytes 4194304 | tf_op jit(solution)/shard_map/neg | solution.py:34
  44.6 1.8 broadcast_divide_fusion
  46.4 12.6 %copy.51 = bf16[8,1,63,2,4096]{4,2,3,0,1:T(8,128)(2,1)} copy(bf16[8,1,63,2,4096]{4,3,2,1,0:T(2,128)(2,1)} %param.3) | data formatting | bytes 16515072 | tf_op args[0]
  59.0 63.6 %multiply_add_fusion = f32[8,48,2,4096]{3,1,2,0:T(8,128)S(1)} fusion(bf16[8,63,2,4096]{3,1,2,0:T(8,128)(2,1)} %bitcast.35, f32[4096]{0:T(1024)S(1)} %get-tuple-element.10, f32[4096]{0:T(1024)S(1)} %get-tuple-element.11, f32[4096]{0:T(1024)S(1)} %get-tuple-element.12, f32[4096]{0:T(1024)S(1)} %get-tuple-element.13, f32[4096]{0:T(1024)S(1)} %get-tuple-element.14, ...), kind=kLoop, calls=%fused_computation.7 | loop fusion | flops 147849216 | bytes 113508352 | tf_op jit(solution)/shard_map/add | solution.py:52
  122.6 12.6 %copy.38 = f32[8,48,2,4096]{3,2,1,0:T(2,128)} copy(f32[8,48,2,4096]{3,1,2,0:T(8,128)S(1)} %multiply_add_fusion) | data formatting | bytes 25165824 | tf_op jit(solution)/shard_map/add | solution.py:52
  135.2 16.9 %reshape.242 = f32[8,48,8192,1]{2,1,0,3:T(8,128)} reshape(f32[8,48,2,4096]{3,2,1,0:T(2,128)} %copy.38) | data formatting | bytes 25165824 | tf_op jit(solution)/shard_map/dot_general | solution.py:37
  152.1 8.9 %maximum_maximum_fusion = f32[8192,512]{0,1:T(8,128)S(1)} fusion(f32[4096,256]{0,1:T(8,128)} %get-tuple-element.28, f32[4096,256]{0,1:T(8,128)} %get-tuple-element.27, f32[4096,256]{0,1:T(8,128)} %fusion.10), kind=kLoop, calls=%fused_computation.3 | loop fusion | flops 12582912 | bytes 29360128 | tf_op jit(solution)/shard_map/concatenate | solution.py:33
  161.0 23.3 %fusion.11 = bf16[8,48,2,256]{3,1,2,0:T(8,128)(2,1)S(1)} fusion(f32[2,256,8192,1]{2,1,0,3:T(8,128)S(1)} %bitcast.36, f32[8,48,8192,1]{2,1,0,3:T(8,128)} %reshape.242), kind=kOutput, calls=%fused_computation.25 | convolution fusion | flops 19327549440 | bytes 29753344 | tf_op jit(solution)/shard_map/dot_general | solution.py:37
  185.3 1.9 gather_fusion
  189.5 1.1 reduce.3
  190.8 1.0 reshape.249
  191.8 16.4 %all-to-all-start = ((bf16[128,2,1152]{2,1,0:T(2,128)(2,1)}), bf16[128,2,1152]{2,1,0:T(2,128)(2,1)S(1)}, u32[]{:S(2)}, u32[]{:S(2)}) async-start(bf16[128,2,1152]{2,1,0:T(2,128)(2,1)} %reshape.249), calls=%async_computation | async-start | bytes 1179648 | tf_op jit(solution)/shard_map/all_to_all | solution.py:64
  208.3 2.4 scatter_custom_fusion
  210.7 20.3 %all-to-all-done = bf16[128,2,1152]{2,1,0:T(2,128)(2,1)S(1)} async-done(((bf16[128,2,1152]{2,1,0:T(2,128)(2,1)}), bf16[128,2,1152]{2,1,0:T(2,128)(2,1)S(1)}, u32[]{:S(2)}, u32[]{:S(2)}) %all-to-all-start) | async-done | bytes 589856 | tf_op jit(solution)/shard_map/all_to_all | solution.py:64
  231.7 1.6 copy.44
  234.3 1.9 copy.46
  238.1 18.8 %all-gather.2.cloned.1.call-done = bf16[3,2,1024,96]{2,1,0,3:T(2,128)(2,1)} async-done(((bf16[3,2,1024,48]{2,1,0,3:T(2,128)(2,1)}), bf16[3,2,1024,96]{2,1,0,3:T(2,128)(2,1)}) %all-gather.2.cloned.1.call-update) | async-done | bytes 1179664 | tf_op jit(solution)/shard_map/all_gather | solution.py:69
  256.9 4.8 %copy.47 = bf16[3,2,1024,96]{3,1,2,0:T(2,128)(2,1)S(1)} copy(bf16[3,2,1024,96]{2,1,0,3:T(2,128)(2,1)} %all-gather.2.cloned.1.call-done) | data formatting | bytes 2359296 | tf_op jit(solution)/shard_map/all_gather | solution.py:69
  261.7 7.2 %gather_fusion.1 = bf16[1024,3,2,96]{3,2,1,0:T(2,128)(2,1)S(1)} fusion(bf16[3,2,1024,96]{3,1,2,0:T(2,128)(2,1)S(1)} %copy.47, s32[1024]{0:T(1024)S(1)} %broadcast_clamp_fusion), kind=kCustom, calls=%fused_computation.1 | custom fusion | bytes 2363392 | tf_op jit(solution)/shard_map/jit(_take)/gather | solution.py:78
  268.9 2.1 copy.48
  271.5 6.4 %fusion.14 = f32[3,1024,1024]{2,1,0:T(8,128)} fusion(bf16[3,1024,96]{1,2,0:T(8,128)(2,1)S(1)} %get-tuple-element.6, bf16[3,1024,96]{1,2,0:T(8,128)(2,1)S(1)} %get-tuple-element.5, bf16[3,512,192]{1,2,0:T(8,128)(2,1)S(1)} %get-tuple-element.8, bf16[3,512,192]{1,2,0:T(8,128)(2,1)S(1)} %get-tuple-element.7), kind=kOutput, calls=%fused_computation.26 | convolution fusion | flops 1212678144 | bytes 14942208 | tf_op jit(solution)/shard_map/kit,kjt->kij/dot_general | solution.py:91
  277.9 9.3 %multiply_convert_fusion = bf16[1,3,2,512,1024]{4,3,2,1,0:T(8,128)(2,1)} fusion(f32[1,3,2,512,1024]{4,3,2,1,0:T(8,128)} %bitcast.37, f32[3]{0:T(128)S(1)} %compare_select_fusion.5), kind=kLoop, calls=%fused_computation.6 | loop fusion | flops 6291456 | bytes 18874380 | tf_op jit(solution)/shard_map/convert_element_type | solution.py:93
  (41 shorter events, 7.7 us)
Async XLA Ops:
  9.0 34.4 %copy-start = (s32[128]{0:T(128)S(1)}, s32[128]{0:T(128)}, u32[]{:S(2)}) copy-start(s32[128]{0:T(128)} %param.5) | copy-start | bytes 1540
  187.2 21.1 %copy-start.1 = (s32[512]{0:T(512)S(1)}, s32[512]{0:T(512)}, u32[]{:S(2)}) copy-start(s32[512]{0:T(512)} %param.4) | copy-start | bytes 6148
  191.8 39.3 %all-to-all-start = ((bf16[128,2,1152]{2,1,0:T(2,128)(2,1)}), bf16[128,2,1152]{2,1,0:T(2,128)(2,1)S(1)}, u32[]{:S(2)}, u32[]{:S(2)}) async-start(bf16[128,2,1152]{2,1,0:T(2,128)(2,1)} %reshape.249), calls=%async_computation | async-start | bytes 1179648 | tf_op jit(solution)/shard_map/all_to_all | solution.py:64
  208.2 48.7 %all-gather.2.cloned.1.call-start = ((), (), s32[]{:S(2)}) async-start(), calls=%async_computation.1 | async-start | bytes 1769472 | tf_op jit(solution)/shard_map/all_gather | solution.py:69
Sparse Core Ops, SparseCore 0:
  236.4 20.4 all-gather.1
where the time goes:
time: 298 us; the launch traced here: 294 us
  other arithmetic  123 us (41%)
  local copies, waits for them, and re-layouts  70.8 us (24%)
  waiting for transfers between devices  39.2 us (13%)
  matrix products  29.7 us (10%)
  starting transfers between devices  16.4 us (6%)
  between operations  14.7 us (5%)
    add x1, other arithmetic, body(): folded + signal[:, tap_idx:tap_idx + NSPEC].astype(jnp.float32) * taper_t...  63.6 us
    dot_general x1, matrix products, direct_dft(): jnp.dot(rows_in, table, precision=lax.Precision.HIGHEST, preferred_elemen...  23.3 us
    all_to_all x1, waiting for transfers between devices, body(): lax.all_to_all(outgoing.reshape(stn_count, -1), 'stn', split_axis=0, conc...  20.3 us
    all_gather x1, waiting for transfers between devices, body(): incoming = lax.all_gather(incoming, 'blk', axis=3, tiled=True)  18.8 us
    sin x1, other arithmetic, direct_dft(): sine = jnp.sin(phase)  17.6 us
    dot_general x1, local copies, waits for them, and re-layouts, direct_dft(): jnp.dot(rows_in, table, precision=lax.Precision.HIGHEST, preferred_elemen...  16.9 us
    neg x1, other arithmetic, direct_dft(): -sine  16.8 us
    all_to_all x1, starting transfers between devices, body(): lax.all_to_all(outgoing.reshape(stn_count, -1), 'stn', split_axis=0, conc...  16.4 us
  transfers between devices with their start and end apart: 2, of which 2 were waited for; matrix products, arithmetic and copies ran while one was open for 1% of the time, Pallas kernels for 0%

commit v1 on v0

v1 whole, which is shorter than its diff:
```python
import functools
import math

import jax
import jax.numpy as jnp
import ml_dtypes
import numpy as np
from jax import lax
from jax.experimental import pallas as pl
from jax.experimental.pallas import tpu as pltpu
from jax.sharding import PartitionSpec as P

FFT_LEN = 4096
TAPS = 16
CAP = 3
NSPEC = 48
FRAMES = 63
STREAMS = 8
BAND = 256
LANES = 128
TILES = FFT_LEN // LANES
STEP_TILES = 2
STEPS = TILES // STEP_TILES
ROWS = NSPEC * STREAMS * 2
SLOTS = 4
CENTRE = (TAPS // 2 - 1, TAPS // 2)
OUTER = sorted((t for t in range(TAPS) if t not in CENTRE), key=lambda t: -abs(t - 7.5))
MESH = pl.DeviceIdType.MESH


def taper_tiles():
    points = np.arange(TAPS * FFT_LEN) + 0.5
    span_len = TAPS * FFT_LEN
    filt = np.sinc((points - span_len / 2) / FFT_LEN) * (
        0.5 - 0.5 * np.cos(2.0 * math.pi * points / span_len)
    )
    filt = filt / np.sqrt(np.sum(filt * filt))
    tiles = filt.reshape(TAPS, TILES, LANES).transpose(1, 0, 2)
    return np.ascontiguousarray(tiles.astype(np.float32))


def dft_table():
    positions = np.arange(FFT_LEN)
    channels = np.arange(BAND)
    phase = (positions[:, None] * channels[None, :] % FFT_LEN) * (2.0 * math.pi / FFT_LEN)
    table = np.concatenate([np.cos(phase), np.sin(phase)], axis=1)
    return table.astype(ml_dtypes.bfloat16)


def fold_step(tap_ref, frames, step, lhs):
    for kk in range(STEP_TILES):
        taps = tap_ref[step * STEP_TILES + kk]
        wide = [jnp.broadcast_to(taps[t : t + 1], (16, LANES)) for t in range(TAPS)]
        low = {t: wide[t].astype(jnp.bfloat16) for t in OUTER}
        volts = [frames[r, kk] for r in range(FRAMES)]
        full = {r: volts[r].astype(jnp.float32) for r in range(CENTRE[0], NSPEC + CENTRE[1])}
        for s in range(NSPEC):
            small = low[OUTER[0]] * volts[s + OUTER[0]]
            for t in OUTER[1:]:
                small = small + low[t] * volts[s + t]
            total = small.astype(jnp.float32)
            for t in CENTRE:
                total = total + wide[t] * full[s + t]
            lhs[s * 16 : (s + 1) * 16, kk * LANES : (kk + 1) * LANES] = total.astype(jnp.bfloat16)


def channelize(volt_ref, tap_ref, table_ref, count_ref, out_ref, frames, tables, lhs_a, lhs_b, acc, spec, wide, sems, table_sems):
    def copies(step):
        slot = lax.rem(step, SLOTS)
        tile = step * STEP_TILES
        made = []
        for a in range(STREAMS):
            made.append(
                pltpu.make_async_copy(
                    volt_ref.at[a, :, pl.ds(tile, STEP_TILES)],
                    frames.at[slot, :, :, a],
                    sems.at[slot, a],
                )
            )
        made.append(
            pltpu.make_async_copy(
                table_ref.at[pl.ds(tile * LANES, STEP_TILES * LANES)],
                tables.at[slot],
                table_sems.at[slot],
            )
        )
        return made

    def start(step):
        for copy in copies(step):
            copy.start()

    def wait(step):
        for copy in copies(step):
            copy.wait()

    view = frames.reshape(SLOTS, FRAMES, STEP_TILES, 16, LANES)

    def fold(step, lhs):
        fold_step(tap_ref, view.at[lax.rem(step, SLOTS)], step, lhs)

    def multiply(step, lhs):
        got = jnp.dot(
            lhs[...], tables[lax.rem(step, SLOTS)], preferred_element_type=jnp.float32
        )
        for q in range(4):
            acc[q] += got[:, q * LANES : (q + 1) * LANES]

    for step in range(3):
        start(step)
    acc[...] = jnp.zeros_like(acc)
    wait(0)
    fold(0, lhs_a)

    def pair(j, carry):
        step = 2 * j
        wait(step + 1)
        start(step + 3)
        fold(step + 1, lhs_b)
        multiply(step, lhs_a)
        wait(step + 2)

        @pl.when(step + 4 < STEPS)
        def _():
            start(step + 4)

        fold(step + 2, lhs_a)
        multiply(step + 1, lhs_b)
        return carry

    lax.fori_loop(0, STEPS // 2 - 1, pair, 0)
    wait(STEPS - 1)
    fold(STEPS - 1, lhs_b)
    multiply(STEPS - 2, lhs_a)
    multiply(STEPS - 1, lhs_b)

    for a in range(STREAMS):
        part = {}
        for p in range(2):
            for q in range(4):
                part[p, q] = acc[q, pl.ds(2 * a + p, NSPEC, stride=16), :]
        for q in range(2):
            cols = slice(q * LANES, (q + 1) * LANES)
            rows = slice(a * NSPEC, (a + 1) * NSPEC)
            spec[0, rows, cols] = (part[0, q] + part[1, q + 2]).astype(jnp.bfloat16)
            spec[1, rows, cols] = (part[1, q] - part[0, q + 2]).astype(jnp.bfloat16)

    row = lax.broadcasted_iota(jnp.int32, (LANES, LANES), 0)
    device = (row & 7) * 16 + (row >> 3)
    lane = lax.broadcasted_iota(jnp.int32, (LANES, LANES), 1)
    counts = jnp.broadcast_to(count_ref[...], (LANES, LANES)).astype(jnp.float32)
    offset = jnp.sum(jnp.where(lane < device, counts, 0.0), axis=1, keepdims=True)
    count = jnp.sum(jnp.where(lane == device, counts, 0.0), axis=1, keepdims=True)
    band = lax.broadcasted_iota(jnp.int32, (LANES, BAND), 1)
    flat = out_ref.reshape(CAP, LANES * 6, LANES)
    for c in range(CAP):
        pick = (offset + jnp.minimum(float(c), count - 1.0)).astype(jnp.int32)
        chosen = jnp.where(band == pick, 1.0, 0.0).astype(jnp.bfloat16)
        for p in range(2):
            turned = lax.dot_general(
                chosen, spec[p], (((1,), (1,)), ((), ())), preferred_element_type=jnp.float32
            )
            for q in range(3):
                wide[pl.ds(2 * q + p, LANES, stride=6), :] = turned[:, q * LANES : (q + 1) * LANES]
        flat[c] = wide[...].astype(jnp.bfloat16)


def run_channelize(voltages, chan_counts):
    tiles = voltages.reshape(STREAMS, FRAMES, 2, TILES, LANES).transpose(0, 1, 3, 2, 4)
    vmem = pl.BlockSpec(memory_space=pltpu.VMEM)
    hbm = pl.BlockSpec(memory_space=pl.ANY)
    return pl.pallas_call(
        channelize,
        out_shape=jax.ShapeDtypeStruct((CAP, 16, 8, 3, 2, LANES), jnp.bfloat16),
        in_specs=[hbm, vmem, hbm, vmem],
        out_specs=vmem,
        scratch_shapes=[
            pltpu.VMEM((SLOTS, FRAMES, STEP_TILES, STREAMS, 2, LANES), jnp.bfloat16),
            pltpu.VMEM((SLOTS, STEP_TILES * LANES, 2 * BAND), jnp.bfloat16),
            pltpu.VMEM((ROWS, STEP_TILES * LANES), jnp.bfloat16),
            pltpu.VMEM((ROWS, STEP_TILES * LANES), jnp.bfloat16),
            pltpu.VMEM((4, ROWS, LANES), jnp.float32),
            pltpu.VMEM((2, ROWS // 2, BAND), jnp.bfloat16),
            pltpu.VMEM((LANES * 6, LANES), jnp.float32),
            pltpu.SemaphoreType.DMA((SLOTS, STREAMS)),
            pltpu.SemaphoreType.DMA((SLOTS,)),
        ],
        compiler_params=pltpu.CompilerParams(vmem_limit_bytes=60 * 1024 * 1024),
        name="channelize",
    )(tiles, jnp.asarray(taper_tiles()), jnp.asarray(dft_table()), chan_counts.reshape(1, LANES))


def corner_turn(sent, got, stage, other, send_z, recv_z, send_x, recv_x, send_y, recv_y, local_sems):
    stn = lax.axis_index("stn")
    blk = lax.axis_index("blk")
    g = lax.rem(stn, 16)
    h = lax.div(stn, 16)
    x = lax.div(h, 2)
    y_hi = lax.rem(h, 2)
    y = 2 * y_hi + blk

    def at(x_to, y_hi_to, g_to):
        return (x_to * 2 + y_hi_to) * 16 + g_to

    near = {"stn": stn, "blk": 1 - blk}
    cross = {"stn": at(x, 1 - y_hi, g), "blk": 1 - blk}
    ring_z = [{"stn": at(x, y_hi, lax.rem(g + j, 16)), "blk": blk} for j in range(1, 16)]
    ring_x = [{"stn": at(lax.rem(x + j, 4), y_hi, g), "blk": blk} for j in range(1, 4)]

    barrier = pltpu.get_barrier_semaphore()
    partners = [*ring_z, *ring_x, near, cross]
    for partner in partners:
        pl.semaphore_signal(barrier, inc=1, device_id=partner, device_id_type=MESH)
    pl.semaphore_wait(barrier, len(partners))

    def remote(src, dst, send, recv, device):
        copy = pltpu.make_async_remote_copy(
            src_ref=src, dst_ref=dst, send_sem=send, recv_sem=recv, device_id=device, device_id_type=MESH
        )
        copy.start()

    def drain(ref, sem):
        pltpu.make_async_copy(ref, ref, sem).wait()

    def own_z(c):
        return pltpu.make_async_copy(sent.at[c, g], stage.at[c, g], local_sems.at[0, c])

    def own_x(c, half):
        if half == 0:
            return pltpu.make_async_copy(
                stage.at[c, :, x * 2 + y_hi], got.at[c, y, x], local_sems.at[1, c]
            )
        return pltpu.make_async_copy(
            stage.at[c, :, x * 2 + 1 - y_hi], other.at[c, x], local_sems.at[2, c]
        )

    def go_z(c):
        own_z(c).start()
        for j in range(1, 16):
            remote(
                sent.at[c, lax.rem(g + j, 16)], stage.at[c, g], send_z.at[c], recv_z.at[c], ring_z[j - 1]
            )

    def go_x(c):
        own_z(c).wait()
        drain(stage.at[c, pl.ds(0, 15)], recv_z.at[c])
        own_x(c, 0).start()
        own_x(c, 1).start()
        for j in range(1, 4):
            x_to = lax.rem(x + j, 4)
            remote(
                stage.at[c, :, x_to * 2 + 1 - y_hi], other.at[c, x], send_x.at[1, c], recv_x.at[1, c], ring_x[j - 1]
            )
        for j in range(1, 4):
            x_to = lax.rem(x + j, 4)
            remote(
                stage.at[c, :, x_to * 2 + y_hi], got.at[c, y, x], send_x.at[0, c], recv_x.at[0, c], ring_x[j - 1]
            )

    def go_y(c):
        own_x(c, 1).wait()
        drain(other.at[c, pl.ds(0, 3)], recv_x.at[1, c])
        remote(other.at[c], got.at[c, y], send_y.at[0, c], recv_y.at[0, c], cross)
        own_x(c, 0).wait()
        drain(other.at[c, pl.ds(0, 3)], recv_x.at[0, c])
        remote(got.at[c, y], got.at[c, y], send_y.at[1, c], recv_y.at[1, c], near)

    def go_forward(c):
        drain(other.at[c], recv_y.at[0, c])
        remote(got.at[c, 3 - y], got.at[c, 3 - y], send_y.at[2, c], recv_y.at[2, c], near)

    for c in range(CAP):
        go_z(c)
    go_x(0)
    go_x(1)
    go_y(0)
    go_x(2)
    go_y(1)
    go_forward(0)
    go_y(2)
    go_forward(1)
    go_forward(2)
    for c in range(CAP):
        for k in (1, 2):
            drain(other.at[c], recv_y.at[k, c])
        drain(stage.at[c, pl.ds(0, 15)], send_z.at[c])
        for k in range(2):
            drain(other.at[c, pl.ds(0, 3)], send_x.at[k, c])
        for k in range(3):
            drain(other.at[c], send_y.at[k, c])


def run_corner_turn(sent):
    vmem = pl.BlockSpec(memory_space=pltpu.VMEM)
    dma = pltpu.SemaphoreType.DMA
    return pl.pallas_call(
        corner_turn,
        out_shape=jax.ShapeDtypeStruct((CAP, 4, 4, 16, 3, 2, LANES), jnp.bfloat16),
        in_specs=[vmem],
        out_specs=vmem,
        scratch_shapes=[
            pltpu.VMEM((CAP, 16, 8, 3, 2, LANES), jnp.bfloat16),
            pltpu.VMEM((CAP, 4, 16, 3, 2, LANES), jnp.bfloat16),
            dma((CAP,)),
            dma((CAP,)),
            dma((2, CAP)),
            dma((2, CAP)),
            dma((3, CAP)),
            dma((3, CAP)),
            dma((3, CAP)),
        ],
        compiler_params=pltpu.CompilerParams(
            collective_id=0, has_side_effects=True, vmem_limit_bytes=16 * 1024 * 1024
        ),
        name="corner_turn",
    )(sent)


HALF = 512
TOTAL = 1024
CHUNK = 128


def correlate(got_ref, map_ref, count_ref, out_ref, places, rows_in, rows, wide):
    c = pl.program_id(0)
    part = pl.program_id(1)

    @pl.when((c == 0) & (part == 0))
    def _():
        want = lax.broadcasted_iota(jnp.int32, (TOTAL, LANES), 0)
        rows_in[...] = jnp.zeros_like(rows_in)
        for a in range(STREAMS):
            row = 2 * map_ref[a // 2 : a // 2 + 1, :] + a % 2
            places[:, a * LANES : (a + 1) * LANES] = jnp.where(want == row, 1.0, 0.0).astype(jnp.bfloat16)

    @pl.when(part == 0)
    def _():
        flat = got_ref.reshape(CAP, TOTAL * 3 // 2, LANES)
        wide[...] = flat[c].astype(jnp.float32)
        for p in range(2):
            for b in range(2):
                pieces = []
                for q in range(3):
                    first = wide[pl.ds(b * 384 + 2 * q + p, 64, stride=6), :]
                    second = wide[pl.ds((b + 2) * 384 + 2 * q + p, 64, stride=6), :]
                    pieces.append(jnp.concatenate([first, second], axis=0))
                line = jnp.concatenate(pieces, axis=1)
                for a in range(STREAMS):
                    lane = p * LANES + b * 64
                    rows_in[a * LANES : (a + 1) * LANES, lane : lane + NSPEC] = line[
                        :, a * NSPEC : (a + 1) * NSPEC
                    ].astype(jnp.bfloat16)
        rows[...] = jnp.dot(
            places[...], rows_in[...], preferred_element_type=jnp.float32
        ).astype(jnp.bfloat16)

    me = lax.axis_index("stn")
    lane = lax.broadcasted_iota(jnp.int32, (1, LANES), 1)
    live = jnp.sum(jnp.where(lane == me, count_ref[...], 0).astype(jnp.float32), axis=1, keepdims=True)
    scale = jnp.where(c.astype(jnp.float32) < live, 1.0 / (2 * NSPEC), 0.0)
    start = pl.multiple_of(lax.axis_index("blk") * HALF + part * CHUNK, CHUNK)
    mine = rows[pl.ds(start, CHUNK), :]
    turned = jnp.concatenate([mine[:, LANES:], -mine[:, :LANES]], axis=1)
    for k, left in enumerate((mine, turned)):
        product = lax.dot_general(
            left, rows[...], (((1,), (1,)), ((), ())), preferred_element_type=jnp.float32
        )
        out_ref[0, 0, k] = (product * scale).astype(jnp.bfloat16)


def run_correlate(got, station_map, chan_counts):
    by_source = station_map.reshape(4, 2, 16, 4).transpose(3, 1, 0, 2).reshape(4, LANES)
    return pl.pallas_call(
        correlate,
        grid=(CAP, HALF // CHUNK),
        out_shape=jax.ShapeDtypeStruct((1, CAP, 2, HALF, TOTAL), jnp.bfloat16),
        in_specs=[
            pl.BlockSpec((CAP, 4, 4, 16, 3, 2, LANES), lambda c, i: (0,) * 7),
            pl.BlockSpec((4, LANES), lambda c, i: (0, 0)),
            pl.BlockSpec((1, LANES), lambda c, i: (0, 0)),
        ],
        out_specs=pl.BlockSpec((1, 1, 2, CHUNK, TOTAL), lambda c, i: (0, c, 0, i, 0)),
        scratch_shapes=[
            pltpu.VMEM((TOTAL, TOTAL), jnp.bfloat16),
            pltpu.VMEM((TOTAL, 2 * LANES), jnp.bfloat16),
            pltpu.VMEM((TOTAL, 2 * LANES), jnp.bfloat16),
            pltpu.VMEM((TOTAL * 3 // 2, LANES), jnp.float32),
        ],
        compiler_params=pltpu.CompilerParams(vmem_limit_bytes=32 * 1024 * 1024),
        name="correlate",
    )(got, by_source, chan_counts.reshape(1, LANES))


def body(voltages, station_map, chan_counts):
    sent = run_channelize(voltages, chan_counts)
    got = run_corner_turn(sent)
    return run_correlate(got, station_map, chan_counts)


def solution(mesh):
    return jax.shard_map(
        body,
        mesh=mesh,
        in_specs=(P("stn", "blk", None, None, None), P(), P()),
        out_specs=P("stn", None, None, "blk", None),
        check_vma=False,
    )
```

time: 298 us -> 78.2 us (0.26)
  the two profiles are of different devices: /device:TPU:1 before, /device:TPU:8 now
where the time goes in v1:
time: 78.2 us; the launch traced here: 77 us
  Pallas kernels  74.9 us (96%)
  local copies, waits for them, and re-layouts  2.05 us (3%)
    pallas_call x1, Pallas kernels, run_corner_turn(): pl.pallas_call(corner_turn, out_shape=jax.ShapeDtypeStruct((CAP, 4, 4, 16...  37.4 us
    pallas_call x1, Pallas kernels, run_channelize(): pl.pallas_call(channelize, out_shape=jax.ShapeDtypeStruct((CAP, 16, 8, 3,...  24.8 us
    pallas_call x1, Pallas kernels, run_correlate(): pl.pallas_call(correlate, grid=(CAP, HALF // CHUNK), out_shape=jax.ShapeD...  12.7 us

profile of v1, /device:TPU:8, one launch (start us, length us, event | category | flops | bytes accessed | tf_op | source)
XLA Modules:
  0.0 77.0 jit_solution(8446897175584167269)
XLA Ops:
  0.0 0.8 %reshape.15 = s32[4,2,16,4]{3,2,1,0:T(8,128)S(1)} reshape(s32[512]{0:T(512)} %param.6) | data formatting | bytes 4096 | tf_op jit(solution)/shard_map/reshape | solution.py:372
  0.8 0.1 copy.6
  0.9 0.1 reshape.16.map_ref
  1.0 0.0 copy-start.1
  1.0 24.8 %channelize.1.sent = bf16[3,16,8,3,2,128]{5,4,3,2,1,0:T(2,128)(2,1)} custom-call(bf16[8,63,32,2,128]{4,3,2,1,0:T(2,128)(2,1)} %bitcast.7, f32[32,16,128]{2,1,0:T(8,128)} %constant.4.clone.tap_ref, bf16[4096,512]{1,0:T(8,128)(2,1)} %constant.5.clone.table_ref, s32[1,128]{1,0:T(1,128)} %bitcast.5), custom_call_target="tpu_custom_call" | custom-call | tf_op jit(solution)/shard_map/channelize/pallas_call | solution.py:172
  25.8 0.0 copy-start
  25.8 1.1 %copy-done = bf16[3,16,8,3,2,128]{5,4,3,2,1,0:T(2,128)(2,1)S(1)} copy-done((bf16[3,16,8,3,2,128]{5,4,3,2,1,0:T(2,128)(2,1)S(1)}, bf16[3,16,8,3,2,128]{5,4,3,2,1,0:T(2,128)(2,1)}, u32[]{:S(2)}) %copy-start) | copy-done | bytes 589848
  26.9 37.4 %corner_turn.1.got_ref = bf16[3,4,4,16,3,2,128]{6,5,4,3,2,1,0:T(2,128)(2,1)S(1)} custom-call(bf16[3,16,8,3,2,128]{5,4,3,2,1,0:T(2,128)(2,1)S(1)} %copy-done), custom_call_target="tpu_custom_call" | custom-call | tf_op jit(solution)/shard_map/corner_turn/pallas_call | solution.py:296
  64.2 0.0 copy-done.1
  64.2 12.7 %correlate.1 = bf16[1,3,2,512,1024]{4,3,2,1,0:T(8,128)(2,1)} custom-call(bf16[3,4,4,16,3,2,128]{6,5,4,3,2,1,0:T(2,128)(2,1)S(1)} %corner_turn.1.got_ref, s32[4,128]{1,0:T(4,128)S(1)} %reshape.16.map_ref, s32[1,128]{1,0:T(1,128)S(1)} %bitcast.6), custom_call_target="tpu_custom_call" | custom-call | tf_op jit(solution)/shard_map/correlate/pallas_call | solution.py:373
Async XLA Ops:
  1.0 63.2 %copy-start.1 = (s32[128]{0:T(128)S(1)}, s32[128]{0:T(128)}, u32[]{:S(2)}) copy-start(s32[128]{0:T(128)} %param.7) | copy-start | bytes 1540
  25.8 1.1 %copy-start = (bf16[3,16,8,3,2,128]{5,4,3,2,1,0:T(2,128)(2,1)S(1)}, bf16[3,16,8,3,2,128]{5,4,3,2,1,0:T(2,128)(2,1)}, u32[]{:S(2)}) copy-start(bf16[3,16,8,3,2,128]{5,4,3,2,1,0:T(2,128)(2,1)} %channelize.1.sent) | copy-start | bytes 1769476

commit v2 on v1

v2 whole, which is shorter than its diff:
```python
import functools
import math

import jax
import jax.numpy as jnp
import ml_dtypes
import numpy as np
from jax import lax
from jax.experimental import pallas as pl
from jax.experimental.pallas import tpu as pltpu
from jax.sharding import PartitionSpec as P

FFT_LEN = 4096
TAPS = 16
CAP = 3
NSPEC = 48
FRAMES = 63
STREAMS = 8
BAND = 256
LANES = 128
TILES = FFT_LEN // LANES
PARTS = 3
SPAN = NSPEC // PARTS
BLOCK = 16
ROWS = SPAN * STREAMS * 2
LAST = TAPS // 2
OUTER = sorted((t for t in range(TAPS) if t not in (LAST - 1, LAST)), key=lambda t: -abs(t - 7.5))
MESH = pl.DeviceIdType.MESH


def prototype():
    points = np.arange(TAPS * FFT_LEN) + 0.5
    span_len = TAPS * FFT_LEN
    filt = np.sinc((points - span_len / 2) / FFT_LEN) * (
        0.5 - 0.5 * np.cos(2.0 * math.pi * points / span_len)
    )
    filt = filt / np.sqrt(np.sum(filt * filt))
    return filt.reshape(TAPS, FFT_LEN)


def tables_of():
    filt = prototype()
    positions = np.arange(FFT_LEN)
    pivot = np.where(positions < FFT_LEN // 2, filt[LAST], filt[LAST - 1])
    ratios = (filt / pivot).reshape(TAPS, TILES, LANES).transpose(1, 0, 2)
    phase = (positions[:, None] * np.arange(BAND)[None, :] % FFT_LEN) * (2.0 * math.pi / FFT_LEN)
    table = np.concatenate([np.cos(phase), np.sin(phase)], axis=1) * pivot[:, None]
    return np.ascontiguousarray(ratios.astype(np.float32)), table.astype(ml_dtypes.bfloat16)


def fold_tile(tap_ref, frames, part, half, tile, lhs):
    pivot, partner = (LAST, LAST - 1) if half == 0 else (LAST - 1, LAST)
    taps = tap_ref[tile]
    low = {
        t: jnp.broadcast_to(taps[t : t + 1], (16, LANES)).astype(jnp.bfloat16)
        for t in [*OUTER, partner]
    }
    lanes = pl.ds(pl.multiple_of(tile * LANES, LANES), LANES)
    for base in range(0, SPAN, BLOCK):
        first = part * SPAN + base
        volts = [frames[first + r, tile] for r in range(BLOCK + TAPS - 1)]
        for s in range(BLOCK):
            small = low[OUTER[0]] * volts[s + OUTER[0]]
            for t in [*OUTER[1:], partner]:
                small = small + low[t] * volts[s + t]
            row = (base + s) * 16
            lhs[row : row + 16, lanes] = volts[s + pivot] + small


def choose_slots(count_ref, chosen):
    row = lax.broadcasted_iota(jnp.int32, (LANES, LANES), 0)
    device = (row & 7) * 16 + (row >> 3)
    lane = lax.broadcasted_iota(jnp.int32, (LANES, LANES), 1)
    counts = jnp.broadcast_to(count_ref[...], (LANES, LANES)).astype(jnp.float32)
    offset = jnp.sum(jnp.where(lane < device, counts, 0.0), axis=1, keepdims=True)
    count = jnp.sum(jnp.where(lane == device, counts, 0.0), axis=1, keepdims=True)
    band = lax.broadcasted_iota(jnp.int32, (LANES, BAND), 1)
    for k in range(CAP):
        pick = (offset + jnp.minimum(float(k), count - 1.0)).astype(jnp.int32)
        chosen[k] = jnp.where(band == pick, 1.0, 0.0).astype(jnp.bfloat16)


def transform(lhs, table, acc):
    got = jnp.dot(lhs[...], table[...], preferred_element_type=jnp.float32)
    for q in range(4):
        acc[q] = got[:, q * LANES : (q + 1) * LANES]


def outgoing(acc, chosen, spec, wide, out):
    for a in range(STREAMS):
        part = {}
        for p in range(2):
            for q in range(4):
                part[p, q] = acc[q, pl.ds(2 * a + p, SPAN, stride=16), :]
        for q in range(2):
            cols = slice(q * LANES, (q + 1) * LANES)
            rows = slice(a * SPAN, (a + 1) * SPAN)
            spec[0, rows, cols] = (part[0, q] + part[1, q + 2]).astype(jnp.bfloat16)
            spec[1, rows, cols] = (part[1, q] - part[0, q + 2]).astype(jnp.bfloat16)
    for k in range(CAP):
        for p in range(2):
            turned = lax.dot_general(
                chosen[k], spec[p], (((1,), (1,)), ((), ())), preferred_element_type=jnp.float32
            )
            wide[pl.ds(2 * k + p, LANES, stride=6), :] = turned
    out.reshape(LANES * 6, LANES)[...] = wide[...].astype(jnp.bfloat16)


def bring_in(volt_ref, out_ref, sems):
    copies = [
        pltpu.make_async_copy(volt_ref.at[a], out_ref.at[:, :, a], sems.at[a]) for a in range(STREAMS)
    ]
    for copy in copies:
        copy.start()
    for copy in copies:
        copy.wait()


def run_bring_in(voltages):
    tiles = voltages.reshape(STREAMS, FRAMES, 2, TILES, LANES).transpose(0, 1, 3, 2, 4)
    frames = pl.pallas_call(
        bring_in,
        out_shape=jax.ShapeDtypeStruct((FRAMES, TILES, STREAMS, 2, LANES), jnp.bfloat16),
        in_specs=[pl.BlockSpec(memory_space=pl.ANY)],
        out_specs=pl.BlockSpec(memory_space=pltpu.VMEM),
        scratch_shapes=[pltpu.SemaphoreType.DMA((STREAMS,))],
        compiler_params=pltpu.CompilerParams(vmem_limit_bytes=42 * 1024 * 1024),
        name="bring_in",
    )(tiles)
    return frames.reshape(FRAMES, TILES, 16, LANES)


class Filter:
    def __init__(self, frames, tap_ref, table, count_ref, lhs, acc, chosen, spec, wide):
        self.args = frames, tap_ref, table, count_ref, lhs, acc, chosen, spec, wide

    def start(self):
        choose_slots(self.args[3], self.args[6])

    def fold(self, part, half):
        frames, tap_ref, lhs = self.args[0], self.args[1], self.args[4]

        def step(i, carry):
            for u in range(2):
                fold_tile(tap_ref, frames, part, half, half * (TILES // 2) + 2 * i + u, lhs)
            return carry

        lax.fori_loop(0, TILES // 4, step, 0)

    def finish(self, out):
        _, _, table, _, lhs, acc, chosen, spec, wide = self.args
        transform(lhs, table, acc)
        outgoing(acc, chosen, spec, wide, out)


FILTER_SCRATCH = [
    pltpu.VMEM((ROWS, FFT_LEN), jnp.bfloat16),
    pltpu.VMEM((4, ROWS, LANES), jnp.float32),
    pltpu.VMEM((CAP, LANES, BAND), jnp.bfloat16),
    pltpu.VMEM((2, ROWS // 2, BAND), jnp.bfloat16),
    pltpu.VMEM((LANES * 6, LANES), jnp.float32),
]


def filter_and_turn(frames, tap_ref, table, count_ref, got, lhs, acc, chosen, spec, wide, sent, stage, other, send_z, recv_z, send_x, recv_x, send_y, recv_y, local_sems):
    stn = lax.axis_index("stn")
    blk = lax.axis_index("blk")
    g = lax.rem(stn, 16)
    h = lax.div(stn, 16)
    x = lax.div(h, 2)
    y_hi = lax.rem(h, 2)
    y = 2 * y_hi + blk

    def at(x_to, y_hi_to, g_to):
        return (x_to * 2 + y_hi_to) * 16 + g_to

    near = {"stn": stn, "blk": 1 - blk}
    cross = {"stn": at(x, 1 - y_hi, g), "blk": 1 - blk}
    ring_z = [{"stn": at(x, y_hi, lax.rem(g + j, 16)), "blk": blk} for j in range(1, 16)]
    ring_x = [{"stn": at(lax.rem(x + j, 4), y_hi, g), "blk": blk} for j in range(1, 4)]

    barrier = pltpu.get_barrier_semaphore()
    partners = [*ring_z, *ring_x, near, cross]
    for partner in partners:
        pl.semaphore_signal(barrier, inc=1, device_id=partner, device_id_type=MESH)
    bank = Filter(frames, tap_ref, table, count_ref, lhs, acc, chosen, spec, wide)

    def remote(src, dst, send, recv, device):
        copy = pltpu.make_async_remote_copy(
            src_ref=src, dst_ref=dst, send_sem=send, recv_sem=recv, device_id=device, device_id_type=MESH
        )
        copy.start()

    def drain(ref, sem):
        pltpu.make_async_copy(ref, ref, sem).wait()

    def own_z(c):
        return pltpu.make_async_copy(sent.at[c, g], stage.at[c, g], local_sems.at[0, c])

    def own_x(c, half):
        if half == 0:
            return pltpu.make_async_copy(
                stage.at[c, :, x * 2 + y_hi], got.at[c, y, x], local_sems.at[1, c]
            )
        return pltpu.make_async_copy(
            stage.at[c, :, x * 2 + 1 - y_hi], other.at[c, x], local_sems.at[2, c]
        )

    def go_z(c):
        own_z(c).start()
        for j in range(1, 16):
            remote(
                sent.at[c, lax.rem(g + j, 16)], stage.at[c, g], send_z.at[c], recv_z.at[c], ring_z[j - 1]
            )

    def go_x(c):
        own_z(c).wait()
        drain(stage.at[c, pl.ds(0, 15)], recv_z.at[c])
        own_x(c, 0).start()
        own_x(c, 1).start()
        for j in range(1, 4):
            x_to = lax.rem(x + j, 4)
            remote(
                stage.at[c, :, x_to * 2 + 1 - y_hi], other.at[c, x], send_x.at[1, c], recv_x.at[1, c], ring_x[j - 1]
            )
        for j in range(1, 4):
            x_to = lax.rem(x + j, 4)
            remote(
                stage.at[c, :, x_to * 2 + y_hi], got.at[c, y, x], send_x.at[0, c], recv_x.at[0, c], ring_x[j - 1]
            )

    def go_y(c):
        own_x(c, 1).wait()
        drain(other.at[c, pl.ds(0, 3)], recv_x.at[1, c])
        remote(other.at[c], got.at[c, y], send_y.at[0, c], recv_y.at[0, c], cross)
        own_x(c, 0).wait()
        drain(other.at[c, pl.ds(0, 3)], recv_x.at[0, c])
        remote(got.at[c, y], got.at[c, y], send_y.at[1, c], recv_y.at[1, c], near)

    def go_forward(c):
        drain(other.at[c], recv_y.at[0, c])
        remote(got.at[c, 3 - y], got.at[c, 3 - y], send_y.at[2, c], recv_y.at[2, c], near)

    bank.start()
    bank.fold(0, 0)
    bank.fold(0, 1)
    bank.finish(sent.at[0])
    pl.semaphore_wait(barrier, len(partners))
    go_z(0)
    bank.fold(1, 0)
    bank.fold(1, 1)
    bank.finish(sent.at[1])
    go_z(1)
    bank.fold(2, 0)
    go_x(0)
    bank.fold(2, 1)
    bank.finish(sent.at[2])
    go_z(2)
    go_y(0)
    go_x(1)
    go_forward(0)
    go_y(1)
    go_x(2)
    go_forward(1)
    go_y(2)
    go_forward(2)
    for c in range(PARTS):
        for k in (1, 2):
            drain(other.at[c], recv_y.at[k, c])
        drain(stage.at[c, pl.ds(0, 15)], send_z.at[c])
        for k in range(2):
            drain(other.at[c, pl.ds(0, 3)], send_x.at[k, c])
        for k in range(3):
            drain(other.at[c], send_y.at[k, c])


def run_filter_and_turn(voltages, chan_counts):
    vmem = pl.BlockSpec(memory_space=pltpu.VMEM)
    dma = pltpu.SemaphoreType.DMA
    ratios, table = tables_of()
    return pl.pallas_call(
        filter_and_turn,
        out_shape=jax.ShapeDtypeStruct((PARTS, 4, 4, 16, CAP, 2, LANES), jnp.bfloat16),
        in_specs=[vmem] * 4,
        out_specs=vmem,
        scratch_shapes=[
            *FILTER_SCRATCH,
            pltpu.VMEM((PARTS, 16, 8, CAP, 2, LANES), jnp.bfloat16),
            pltpu.VMEM((PARTS, 16, 8, CAP, 2, LANES), jnp.bfloat16),
            pltpu.VMEM((PARTS, 4, 16, CAP, 2, LANES), jnp.bfloat16),
            dma((PARTS,)),
            dma((PARTS,)),
            dma((2, PARTS)),
            dma((2, PARTS)),
            dma((3, PARTS)),
            dma((3, PARTS)),
            dma((3, PARTS)),
        ],
        compiler_params=pltpu.CompilerParams(
            collective_id=0, has_side_effects=True, vmem_limit_bytes=16 * 1024 * 1024
        ),
        name="filter_and_turn",
    )(run_bring_in(voltages), jnp.asarray(ratios), jnp.asarray(table), chan_counts.reshape(1, LANES))


HALF = 512
TOTAL = 1024
CHUNK = 128
TIMES = 2 * NSPEC


def correlate(got_ref, map_ref, count_ref, out_ref, places, wide, lines, columns, mine, turned):
    k = pl.program_id(0)
    part = pl.program_id(1)

    @pl.when((k == 0) & (part == 0))
    def _():
        want = lax.broadcasted_iota(jnp.int32, (LANES, TOTAL), 1)
        for a in range(STREAMS):
            row = 2 * map_ref[:, a // 2 : a // 2 + 1] + a % 2
            places[a * LANES : (a + 1) * LANES, :] = jnp.where(want == row, 1.0, 0.0).astype(jnp.bfloat16)
        wide[...] = got_ref[...].astype(jnp.float32)

    @pl.when(part == 0)
    def _():
        for p in range(2):
            for b in range(2):
                for t in range(PARTS):
                    base = t * 1536 + 2 * k + p
                    first = wide[pl.ds(base + b * 384, 64, stride=6), :]
                    second = wide[pl.ds(base + (b + 2) * 384, 64, stride=6), :]
                    block = jnp.concatenate([first, second], axis=0).T.astype(jnp.bfloat16)
                    row = p * TIMES + b * NSPEC + t * SPAN
                    for a in range(STREAMS):
                        lines[row : row + SPAN, a * LANES : (a + 1) * LANES] = block[
                            a * SPAN : (a + 1) * SPAN
                        ]
        ordered = jnp.dot(lines[...], places[...], preferred_element_type=jnp.float32)
        columns[...] = ordered.astype(jnp.bfloat16)
        start = pl.multiple_of(lax.axis_index("blk") * HALF, HALF)
        near = columns[:, pl.ds(start, HALF)].astype(jnp.float32)
        mine[...] = near.T.astype(jnp.bfloat16)
        turned[...] = jnp.concatenate([near[TIMES:], -near[:TIMES]], axis=0).T.astype(jnp.bfloat16)

    me = lax.axis_index("stn")
    lane = lax.broadcasted_iota(jnp.int32, (1, LANES), 1)
    live = jnp.sum(jnp.where(lane == me, count_ref[...], 0).astype(jnp.float32), axis=1, keepdims=True)
    scale = jnp.where(k.astype(jnp.float32) < live, 1.0 / TIMES, 0.0)
    rows = pl.ds(pl.multiple_of(part * CHUNK, CHUNK), CHUNK)
    for i, left in enumerate((mine, turned)):
        product = jnp.dot(left[rows, :], columns[...], preferred_element_type=jnp.float32)
        out_ref[0, 0, i] = (product * scale).astype(jnp.bfloat16)


def run_correlate(got, station_map, chan_counts):
    by_source = station_map.reshape(4, 2, 16, 4).transpose(1, 0, 2, 3).reshape(LANES, 4)
    return pl.pallas_call(
        correlate,
        grid=(CAP, HALF // CHUNK),
        out_shape=jax.ShapeDtypeStruct((1, CAP, 2, HALF, TOTAL), jnp.bfloat16),
        in_specs=[
            pl.BlockSpec((PARTS * TOTAL * 3 // 2, LANES), lambda k, i: (0, 0)),
            pl.BlockSpec((LANES, 4), lambda k, i: (0, 0)),
            pl.BlockSpec((1, LANES), lambda k, i: (0, 0)),
        ],
        out_specs=pl.BlockSpec((1, 1, 2, CHUNK, TOTAL), lambda k, i: (0, k, 0, i, 0)),
        scratch_shapes=[
            pltpu.VMEM((TOTAL, TOTAL), jnp.bfloat16),
            pltpu.VMEM((PARTS * TOTAL * 3 // 2, LANES), jnp.float32),
            pltpu.VMEM((2 * TIMES, TOTAL), jnp.bfloat16),
            pltpu.VMEM((2 * TIMES, TOTAL), jnp.bfloat16),
            pltpu.VMEM((HALF, 2 * TIMES), jnp.bfloat16),
            pltpu.VMEM((HALF, 2 * TIMES), jnp.bfloat16),
        ],
        compiler_params=pltpu.CompilerParams(vmem_limit_bytes=32 * 1024 * 1024),
        name="correlate",
    )(got.reshape(PARTS * TOTAL * 3 // 2, LANES), by_source, chan_counts.reshape(1, LANES))


def body(voltages, station_map, chan_counts):
    got = run_filter_and_turn(voltages, chan_counts)
    return run_correlate(got, station_map, chan_counts)


def solution(mesh):
    return jax.shard_map(
        body,
        mesh=mesh,
        in_specs=(P("stn", "blk", None, None, None), P(), P()),
        out_specs=P("stn", None, None, "blk", None),
        check_vma=False,
    )
```

time: 78.2 us -> 54.9 us (0.70); the launches traced: 77 us -> 54.8 us
  Pallas kernels: 74.9 us -> 53.6 us
  local copies, waits for them, and re-layouts: 2.05 us -> 1.17 us
    pallas_call x2, Pallas kernels: 62.1 us -> 43.5 us  [the longest x1 40 us: run_filter_and_turn(): pl.pallas_call(filter_and_turn, out_shape=jax.ShapeDtypeStruct((PARTS, 4,...]
    pallas_call x1, Pallas kernels: 12.7 us -> 10.1 us  [run_correlate(): pl.pallas_call(correlate, grid=(CAP, HALF // CHUNK), out_shape=jax.ShapeD...]
where the time goes in v2:
time: 54.9 us; the launch traced here: 54.8 us
  Pallas kernels  53.6 us (98%)
  local copies, waits for them, and re-layouts  1.17 us (2%)
    pallas_call x1, Pallas kernels, run_filter_and_turn(): pl.pallas_call(filter_and_turn, out_shape=jax.ShapeDtypeStruct((PARTS, 4,...  40 us
    pallas_call x1, Pallas kernels, run_correlate(): pl.pallas_call(correlate, grid=(CAP, HALF // CHUNK), out_shape=jax.ShapeD...  10.1 us
    pallas_call x1, Pallas kernels, run_bring_in(): pl.pallas_call(bring_in, out_shape=jax.ShapeDtypeStruct((FRAMES, TILES, S...  3.58 us

profile of v2, /device:TPU:8, one launch (start us, length us, event | category | flops | bytes accessed | tf_op | source)
XLA Modules:
  0.0 54.8 jit_solution(17795819563885706273)
XLA Ops:
  0.0 0.0 copy-start
  0.0 0.0 copy-start.1
  0.0 0.0 copy-start.2
  0.0 3.6 %bring_in.1 = bf16[63,32,8,2,128]{4,3,2,1,0:T(2,128)(2,1)S(1)} custom-call(bf16[8,63,32,2,128]{4,3,2,1,0:T(2,128)(2,1)} %bitcast.13), custom_call_target="tpu_custom_call" | custom-call | tf_op jit(solution)/shard_map/bring_in/pallas_call | solution.py:121
  3.6 1.0 %copy-done = bf16[4096,512]{1,0:T(8,128)(2,1)S(1)} copy-done((bf16[4096,512]{1,0:T(8,128)(2,1)S(1)}, bf16[4096,512]{1,0:T(8,128)(2,1)}, u32[]{:S(2)}) %copy-start) | copy-done | bytes 4194328
  4.6 0.0 copy-done.1
  4.6 0.0 copy-done.2
  4.6 0.0 copy-start.3
  4.6 40.0 %filter_and_turn.1 = bf16[3,4,4,16,3,2,128]{6,5,4,3,2,1,0:T(2,128)(2,1)S(1)} custom-call(bf16[63,32,16,128]{3,2,1,0:T(8,128)(2,1)S(1)} %bitcast.8, f32[32,16,128]{2,1,0:T(8,128)S(1)} %copy-done.1, bf16[4096,512]{1,0:T(8,128)(2,1)S(1)} %copy-done, s32[1,128]{1,0:T(1,128)S(1)} %bitcast.11), custom_call_target="tpu_custom_call" | custom-call | tf_op jit(solution)/shard_map/filter_and_turn/pallas_call | solution.py:281
  44.6 0.0 copy-done.3
  44.6 0.1 reshape.23
  44.7 10.1 %correlate.1 = bf16[1,3,2,512,1024]{4,3,2,1,0:T(8,128)(2,1)} custom-call(bf16[4608,128]{1,0:T(8,128)(2,1)S(1)} %bitcast.9, s32[128,4]{1,0:T(8,128)S(1)} %bitcast.10, s32[1,128]{1,0:T(1,128)S(1)} %bitcast.12), custom_call_target="tpu_custom_call" | custom-call | tf_op jit(solution)/shard_map/correlate/pallas_call | solution.py:357
  (1 shorter events, 0.0 us)
Async XLA Ops:
  0.0 4.6 %copy-start = (bf16[4096,512]{1,0:T(8,128)(2,1)S(1)}, bf16[4096,512]{1,0:T(8,128)(2,1)}, u32[]{:S(2)}) copy-start(bf16[4096,512]{1,0:T(8,128)(2,1)} %constant.5.clone.table) | copy-start | bytes 12582916
  0.0 4.6 %copy-start.1 = (f32[32,16,128]{2,1,0:T(8,128)S(1)}, f32[32,16,128]{2,1,0:T(8,128)}, u32[]{:S(2)}) copy-start(f32[32,16,128]{2,1,0:T(8,128)} %constant.4.clone.tap_ref) | copy-start | bytes 786436
  0.0 4.6 %copy-start.2 = (s32[128]{0:T(128)S(1)}, s32[128]{0:T(128)}, u32[]{:S(2)}) copy-start(s32[128]{0:T(128)} %param.7) | copy-start | bytes 1540
  4.6 40.0 %copy-start.3 = (s32[512]{0:T(512)S(1)}, s32[512]{0:T(512)}, u32[]{:S(2)}) copy-start(s32[512]{0:T(512)} %param.6) | copy-start | bytes 6148

commit v3 on v2

--- a/solution.py
+++ b/solution.py
@@ -162,7 +162,49 @@
 ]
 
 
-def filter_and_turn(frames, tap_ref, table, count_ref, got, lhs, acc, chosen, spec, wide, sent, stage, other, send_z, recv_z, send_x, recv_x, send_y, recv_y, local_sems):
+HALF = 512
+TOTAL = 1024
+TIMES = 2 * NSPEC
+LINES = TOTAL * 3 // 2
+
+
+def build_places(map_ref, places):
+    row = lax.broadcasted_iota(jnp.int32, (LANES, LANES), 0)
+    lane = lax.broadcasted_iota(jnp.int32, (LANES, LANES), 1)
+    listed = jnp.zeros((LANES, LANES), jnp.float32)
+    for x in range(4):
+        stations = jnp.broadcast_to(map_ref[x : x + 1, :], (LANES, LANES)).astype(jnp.float32)
+        listed = jnp.where(((row >> 4) & 3) == x, stations, listed)
+    first = (row >> 6) * 64 + (row & 15) * 4
+    want = lax.broadcasted_iota(jnp.int32, (LANES, TOTAL), 1)
+    for pair in range(4):
+        station = jnp.sum(jnp.where(lane == first + pair, listed, 0.0), axis=1, keepdims=True)
+        for p in range(2):
+            a = 2 * pair + p
+            target = 2 * station.astype(jnp.int32) + p
+            places[a * LANES : (a + 1) * LANES, :] = jnp.where(want == target, 1.0, 0.0).astype(jnp.bfloat16)
+
+
+def order_rows(part, got, places, gathered, lines, columns):
+    gathered[...] = got.reshape(LINES, LANES)[...].astype(jnp.float32)
+    spots = [(k, p, b) for k in range(CAP) for p in range(2) for b in range(2)]
+    for i, (k, p, b) in enumerate(spots):
+        base = 2 * k + p
+        first = gathered[pl.ds(base + b * 384, 64, stride=6), :]
+        second = gathered[pl.ds(base + (b + 2) * 384, 64, stride=6), :]
+        block = jnp.concatenate([first, second], axis=0).T.astype(jnp.bfloat16)
+        for a in range(STREAMS):
+            lines[i * SPAN : (i + 1) * SPAN, a * LANES : (a + 1) * LANES] = block[a * SPAN : (a + 1) * SPAN]
+    ordered = jnp.dot(lines[...], places[...], preferred_element_type=jnp.float32)
+    for i, (k, p, b) in enumerate(spots):
+        row = p * TIMES + b * NSPEC + part * SPAN
+        columns[k, row : row + SPAN, :] = ordered[i * SPAN : (i + 1) * SPAN].astype(jnp.bfloat16)
+
+
+def filter_and_turn(
+    frames, tap_ref, table, count_ref, map_ref, columns, lhs, acc, chosen, spec, wide, places, gathered,
+    lines, got, sent, stage, other, send_z, recv_z, send_x, recv_x, send_y, recv_y, local_sems
+):
     stn = lax.axis_index("stn")
     blk = lax.axis_index("blk")
     g = lax.rem(stn, 16)
@@ -240,6 +282,11 @@
     def go_forward(c):
         drain(other.at[c], recv_y.at[0, c])
         remote(got.at[c, 3 - y], got.at[c, 3 - y], send_y.at[2, c], recv_y.at[2, c], near)
+
+    def order(c):
+        drain(other.at[c], recv_y.at[1, c])
+        drain(other.at[c], recv_y.at[2, c])
+        order_rows(c, got.at[c], places, gathered, lines, columns)
 
     bank.start()
     bank.fold(0, 0)
@@ -257,6 +304,7 @@
     bank.finish(sent.at[2])
     go_z(2)
     go_y(0)
+    build_places(map_ref, places)
     go_x(1)
     go_forward(0)
     go_y(1)
@@ -265,8 +313,8 @@
     go_y(2)
     go_forward(2)
     for c in range(PARTS):
-        for k in (1, 2):
-            drain(other.at[c], recv_y.at[k, c])
+        order(c)
+    for c in range(PARTS):
         drain(stage.at[c, pl.ds(0, 15)], send_z.at[c])
         for k in range(2):
             drain(other.at[c, pl.ds(0, 3)], send_x.at[k, c])
@@ -274,17 +322,21 @@
             drain(other.at[c], send_y.at[k, c])
 
 
-def run_filter_and_turn(voltages, chan_counts):
+def run_filter_and_turn(voltages, station_map, chan_counts):
     vmem = pl.BlockSpec(memory_space=pltpu.VMEM)
     dma = pltpu.SemaphoreType.DMA
     ratios, table = tables_of()
     return pl.pallas_call(
         filter_and_turn,
-        out_shape=jax.ShapeDtypeStruct((PARTS, 4, 4, 16, CAP, 2, LANES), jnp.bfloat16),
-        in_specs=[vmem] * 4,
+        out_shape=jax.ShapeDtypeStruct((CAP, 2 * TIMES, TOTAL), jnp.bfloat16),
+        in_specs=[vmem] * 5,
         out_specs=vmem,
         scratch_shapes=[
             *FILTER_SCRATCH,
+            pltpu.VMEM((TOTAL, TOTAL), jnp.bfloat16),
+            pltpu.VMEM((LINES, LANES), jnp.float32),
+            pltpu.VMEM((12 * SPAN, TOTAL), jnp.bfloat16),
+            pltpu.VMEM((PARTS, 4, 4, 16, CAP, 2, LANES), jnp.bfloat16),
             pltpu.VMEM((PARTS, 16, 8, CAP, 2, LANES), jnp.bfloat16),
             pltpu.VMEM((PARTS, 16, 8, CAP, 2, LANES), jnp.bfloat16),
             pltpu.VMEM((PARTS, 4, 16, CAP, 2, LANES), jnp.bfloat16),
@@ -297,89 +349,62 @@
             dma((3, PARTS)),
         ],
         compiler_params=pltpu.CompilerParams(
-            collective_id=0, has_side_effects=True, vmem_limit_bytes=16 * 1024 * 1024
+            collective_id=0, has_side_effects=True, vmem_limit_bytes=24 * 1024 * 1024
         ),
         name="filter_and_turn",
-    )(run_bring_in(voltages), jnp.asarray(ratios), jnp.asarray(table), chan_counts.reshape(1, LANES))
-
-
-HALF = 512
-TOTAL = 1024
-CHUNK = 128
-TIMES = 2 * NSPEC
-
-
-def correlate(got_ref, map_ref, count_ref, out_ref, places, wide, lines, columns, mine, turned):
+    )(
+        run_bring_in(voltages),
+        jnp.asarray(ratios),
+        jnp.asarray(table),
+        chan_counts.reshape(1, LANES),
+        station_map.reshape(4, LANES),
+    )
+
+
+COLUMNS = 512
+
+
+def correlate(columns, count_ref, out_ref, left):
     k = pl.program_id(0)
     part = pl.program_id(1)
 
-    @pl.when((k == 0) & (part == 0))
-    def _():
-        want = lax.broadcasted_iota(jnp.int32, (LANES, TOTAL), 1)
-        for a in range(STREAMS):
-            row = 2 * map_ref[:, a // 2 : a // 2 + 1] + a % 2
-            places[a * LANES : (a + 1) * LANES, :] = jnp.where(want == row, 1.0, 0.0).astype(jnp.bfloat16)
-        wide[...] = got_ref[...].astype(jnp.float32)
-
     @pl.when(part == 0)
     def _():
-        for p in range(2):
-            for b in range(2):
-                for t in range(PARTS):
-                    base = t * 1536 + 2 * k + p
-                    first = wide[pl.ds(base + b * 384, 64, stride=6), :]
-                    second = wide[pl.ds(base + (b + 2) * 384, 64, stride=6), :]
-                    block = jnp.concatenate([first, second], axis=0).T.astype(jnp.bfloat16)
-                    row = p * TIMES + b * NSPEC + t * SPAN
-                    for a in range(STREAMS):
-                        lines[row : row + SPAN, a * LANES : (a + 1) * LANES] = block[
-                            a * SPAN : (a + 1) * SPAN
-                        ]
-        ordered = jnp.dot(lines[...], places[...], preferred_element_type=jnp.float32)
-        columns[...] = ordered.astype(jnp.bfloat16)
         start = pl.multiple_of(lax.axis_index("blk") * HALF, HALF)
-        near = columns[:, pl.ds(start, HALF)].astype(jnp.float32)
-        mine[...] = near.T.astype(jnp.bfloat16)
-        turned[...] = jnp.concatenate([near[TIMES:], -near[:TIMES]], axis=0).T.astype(jnp.bfloat16)
+        mine = columns[k, :, pl.ds(start, HALF)]
+        left[:HALF, :] = mine.T
+        left[HALF:, :] = jnp.concatenate([mine[TIMES:], -mine[:TIMES]], axis=0).T
 
     me = lax.axis_index("stn")
     lane = lax.broadcasted_iota(jnp.int32, (1, LANES), 1)
     live = jnp.sum(jnp.where(lane == me, count_ref[...], 0).astype(jnp.float32), axis=1, keepdims=True)
     scale = jnp.where(k.astype(jnp.float32) < live, 1.0 / TIMES, 0.0)
-    rows = pl.ds(pl.multiple_of(part * CHUNK, CHUNK), CHUNK)
-    for i, left in enumerate((mine, turned)):
-        product = jnp.dot(left[rows, :], columns[...], preferred_element_type=jnp.float32)
-        out_ref[0, 0, i] = (product * scale).astype(jnp.bfloat16)
-
-
-def run_correlate(got, station_map, chan_counts):
-    by_source = station_map.reshape(4, 2, 16, 4).transpose(1, 0, 2, 3).reshape(LANES, 4)
+    for n in range(COLUMNS // 256):
+        right = columns[k, :, pl.ds(pl.multiple_of(part * COLUMNS + n * 256, 256), 256)]
+        for i in range(2):
+            product = jnp.dot(left[i * HALF : (i + 1) * HALF], right, preferred_element_type=jnp.float32)
+            out_ref[0, 0, i, :, n * 256 : (n + 1) * 256] = (product * scale).astype(jnp.bfloat16)
+
+
+def run_correlate(columns, chan_counts):
     return pl.pallas_call(
         correlate,
-        grid=(CAP, HALF // CHUNK),
+        grid=(CAP, TOTAL // COLUMNS),
         out_shape=jax.ShapeDtypeStruct((1, CAP, 2, HALF, TOTAL), jnp.bfloat16),
         in_specs=[
-            pl.BlockSpec((PARTS * TOTAL * 3 // 2, LANES), lambda k, i: (0, 0)),
-            pl.BlockSpec((LANES, 4), lambda k, i: (0, 0)),
-            pl.BlockSpec((1, LANES), lambda k, i: (0, 0)),
+            pl.BlockSpec(memory_space=pltpu.VMEM),
+            pl.BlockSpec(memory_space=pltpu.VMEM),
         ],
-        out_specs=pl.BlockSpec((1, 1, 2, CHUNK, TOTAL), lambda k, i: (0, k, 0, i, 0)),
-        scratch_shapes=[
-            pltpu.VMEM((TOTAL, TOTAL), jnp.bfloat16),
-            pltpu.VMEM((PARTS * TOTAL * 3 // 2, LANES), jnp.float32),
-            pltpu.VMEM((2 * TIMES, TOTAL), jnp.bfloat16),
-            pltpu.VMEM((2 * TIMES, TOTAL), jnp.bfloat16),
-            pltpu.VMEM((HALF, 2 * TIMES), jnp.bfloat16),
-            pltpu.VMEM((HALF, 2 * TIMES), jnp.bfloat16),
-        ],
+        out_specs=pl.BlockSpec((1, 1, 2, HALF, COLUMNS), lambda k, i: (0, k, 0, 0, i)),
+        scratch_shapes=[pltpu.VMEM((TOTAL, 2 * TIMES), jnp.bfloat16)],
         compiler_params=pltpu.CompilerParams(vmem_limit_bytes=32 * 1024 * 1024),
         name="correlate",
-    )(got.reshape(PARTS * TOTAL * 3 // 2, LANES), by_source, chan_counts.reshape(1, LANES))
+    )(columns, chan_counts.reshape(1, LANES))
 
 
 def body(voltages, station_map, chan_counts):
-    got = run_filter_and_turn(voltages, chan_counts)
-    return run_correlate(got, station_map, chan_counts)
+    columns = run_filter_and_turn(voltages, station_map, chan_counts)
+    return run_correlate(columns, chan_counts)
 
 
 def solution(mesh):

time: 54.9 us -> 51.3 us (0.934)
  Pallas kernels: 53.6 us -> 50.2 us
    pallas_call x2, Pallas kernels: 50 us -> 46.6 us  [the longest x1 41.3 us: run_filter_and_turn(): pl.pallas_call(filter_and_turn, out_shape=jax.ShapeDtypeStruct((CAP, 2 *...]
where the time goes in v3:
time: 51.3 us; the launch traced here: 51.2 us
  Pallas kernels  50.2 us (98%)
  local copies, waits for them, and re-layouts  1.05 us (2%)
    pallas_call x1, Pallas kernels, run_filter_and_turn(): pl.pallas_call(filter_and_turn, out_shape=jax.ShapeDtypeStruct((CAP, 2 *...  41.3 us
    pallas_call x1, Pallas kernels, run_correlate(): pl.pallas_call(correlate, grid=(CAP, TOTAL // COLUMNS), out_shape=jax.Sha...  5.31 us
    pallas_call x1, Pallas kernels, run_bring_in(): pl.pallas_call(bring_in, out_shape=jax.ShapeDtypeStruct((FRAMES, TILES, S...  3.58 us
    unnamed x8, local copies, waits for them, and re-layouts  1.05 us

profile of v3, /device:TPU:8, one launch (start us, length us, event | category | flops | bytes accessed | tf_op | source)
XLA Modules:
  0.0 51.2 jit_solution(11320155377885440931)
XLA Ops:
  0.0 0.0 copy-start
  0.0 0.0 copy-start.1
  0.0 0.0 copy-start.2
  0.0 0.0 copy-start.3
  0.0 3.6 %bring_in.1 = bf16[63,32,8,2,128]{4,3,2,1,0:T(2,128)(2,1)S(1)} custom-call(bf16[8,63,32,2,128]{4,3,2,1,0:T(2,128)(2,1)} %bitcast.10), custom_call_target="tpu_custom_call" | custom-call | tf_op jit(solution)/shard_map/bring_in/pallas_call | solution.py:121
  3.6 1.0 %copy-done = bf16[4096,512]{1,0:T(8,128)(2,1)S(1)} copy-done((bf16[4096,512]{1,0:T(8,128)(2,1)S(1)}, bf16[4096,512]{1,0:T(8,128)(2,1)}, u32[]{:S(2)}) %copy-start) | copy-done | bytes 4194328
  4.6 0.0 copy-done.1
  4.6 0.0 copy-done.2
  4.6 0.0 copy-done.3
  4.6 41.3 %filter_and_turn.1.columns = bf16[3,192,1024]{2,1,0:T(8,128)(2,1)S(1)} custom-call(bf16[63,32,16,128]{3,2,1,0:T(8,128)(2,1)S(1)} %bitcast.6, f32[32,16,128]{2,1,0:T(8,128)S(1)} %copy-done.1, bf16[4096,512]{1,0:T(8,128)(2,1)S(1)} %copy-done, s32[1,128]{1,0:T(1,128)S(1)} %bitcast.8, s32[4,128]{1,0:T(4,128)S(1)} %bitcast.7), custom_call_target="tpu_custom_call" | custom-call | tf_op jit(solution)/shard_map/filter_and_turn/pallas_call | solution.py:329
  45.9 5.3 %correlate.1 = bf16[1,3,2,512,1024]{4,3,2,1,0:T(8,128)(2,1)} custom-call(bf16[3,192,1024]{2,1,0:T(8,128)(2,1)S(1)} %filter_and_turn.1.columns, s32[1,128]{1,0:T(1,128)S(1)} %bitcast.9), custom_call_target="tpu_custom_call" | custom-call | tf_op jit(solution)/shard_map/correlate/pallas_call | solution.py:390
Async XLA Ops:
  0.0 4.6 %copy-start = (bf16[4096,512]{1,0:T(8,128)(2,1)S(1)}, bf16[4096,512]{1,0:T(8,128)(2,1)}, u32[]{:S(2)}) copy-start(bf16[4096,512]{1,0:T(8,128)(2,1)} %constant.5.clone.table) | copy-start | bytes 12582916
  0.0 4.6 %copy-start.1 = (f32[32,16,128]{2,1,0:T(8,128)S(1)}, f32[32,16,128]{2,1,0:T(8,128)}, u32[]{:S(2)}) copy-start(f32[32,16,128]{2,1,0:T(8,128)} %constant.4.clone.tap_ref) | copy-start | bytes 786436
  0.0 4.6 %copy-start.2 = (s32[512]{0:T(512)S(1)}, s32[512]{0:T(512)}, u32[]{:S(2)}) copy-start(s32[512]{0:T(512)} %param.6) | copy-start | bytes 6148
  0.0 4.6 %copy-start.3 = (s32[128]{0:T(128)S(1)}, s32[128]{0:T(128)}, u32[]{:S(2)}) copy-start(s32[128]{0:T(128)} %param.7) | copy-start | bytes 1540

commit v4 on v3

--- a/solution.py
+++ b/solution.py
@@ -202,8 +202,8 @@
 
 
 def filter_and_turn(
-    frames, tap_ref, table, count_ref, map_ref, columns, lhs, acc, chosen, spec, wide, places, gathered,
-    lines, got, sent, stage, other, send_z, recv_z, send_x, recv_x, send_y, recv_y, local_sems
+    frames, tap_ref, table_ref, count_ref, map_ref, columns, lhs, acc, chosen, spec, wide, table, places, gathered,
+    lines, got, sent, stage, other, table_sem, send_z, recv_z, send_x, recv_x, send_y, recv_y, local_sems
 ):
     stn = lax.axis_index("stn")
     blk = lax.axis_index("blk")
@@ -225,6 +225,8 @@
     partners = [*ring_z, *ring_x, near, cross]
     for partner in partners:
         pl.semaphore_signal(barrier, inc=1, device_id=partner, device_id_type=MESH)
+    load_table = pltpu.make_async_copy(table_ref.at[pl.ds(0, FFT_LEN)], table, table_sem.at[0])
+    load_table.start()
     bank = Filter(frames, tap_ref, table, count_ref, lhs, acc, chosen, spec, wide)
 
     def remote(src, dst, send, recv, device):
@@ -250,7 +252,7 @@
 
     def go_z(c):
         own_z(c).start()
-        for j in range(1, 16):
+        for j in (8, 7, 9, 6, 10, 5, 11, 4, 12, 3, 13, 2, 14, 1, 15):
             remote(
                 sent.at[c, lax.rem(g + j, 16)], stage.at[c, g], send_z.at[c], recv_z.at[c], ring_z[j - 1]
             )
@@ -291,6 +293,7 @@
     bank.start()
     bank.fold(0, 0)
     bank.fold(0, 1)
+    load_table.wait()
     bank.finish(sent.at[0])
     pl.semaphore_wait(barrier, len(partners))
     go_z(0)
@@ -326,13 +329,15 @@
     vmem = pl.BlockSpec(memory_space=pltpu.VMEM)
     dma = pltpu.SemaphoreType.DMA
     ratios, table = tables_of()
+    padded = np.pad(table, ((0, 3 * FFT_LEN), (0, 0)))
     return pl.pallas_call(
         filter_and_turn,
         out_shape=jax.ShapeDtypeStruct((CAP, 2 * TIMES, TOTAL), jnp.bfloat16),
-        in_specs=[vmem] * 5,
+        in_specs=[vmem, vmem, pl.BlockSpec(memory_space=pl.ANY), vmem, vmem],
         out_specs=vmem,
         scratch_shapes=[
             *FILTER_SCRATCH,
+            pltpu.VMEM((FFT_LEN, 2 * BAND), jnp.bfloat16),
             pltpu.VMEM((TOTAL, TOTAL), jnp.bfloat16),
             pltpu.VMEM((LINES, LANES), jnp.float32),
             pltpu.VMEM((12 * SPAN, TOTAL), jnp.bfloat16),
@@ -340,6 +345,7 @@
             pltpu.VMEM((PARTS, 16, 8, CAP, 2, LANES), jnp.bfloat16),
             pltpu.VMEM((PARTS, 16, 8, CAP, 2, LANES), jnp.bfloat16),
             pltpu.VMEM((PARTS, 4, 16, CAP, 2, LANES), jnp.bfloat16),
+            dma((1,)),
             dma((PARTS,)),
             dma((PARTS,)),
             dma((2, PARTS)),
@@ -349,13 +355,13 @@
             dma((3, PARTS)),
         ],
         compiler_params=pltpu.CompilerParams(
-            collective_id=0, has_side_effects=True, vmem_limit_bytes=24 * 1024 * 1024
+            collective_id=0, has_side_effects=True, vmem_limit_bytes=36 * 1024 * 1024
         ),
         name="filter_and_turn",
     )(
         run_bring_in(voltages),
         jnp.asarray(ratios),
-        jnp.asarray(table),
+        jnp.asarray(padded),
         chan_counts.reshape(1, LANES),
         station_map.reshape(4, LANES),
     )
@@ -372,8 +378,7 @@
     def _():
         start = pl.multiple_of(lax.axis_index("blk") * HALF, HALF)
         mine = columns[k, :, pl.ds(start, HALF)]
-        left[:HALF, :] = mine.T
-        left[HALF:, :] = jnp.concatenate([mine[TIMES:], -mine[:TIMES]], axis=0).T
+        left[...] = mine.T
 
     me = lax.axis_index("stn")
     lane = lax.broadcasted_iota(jnp.int32, (1, LANES), 1)
@@ -381,8 +386,9 @@
     scale = jnp.where(k.astype(jnp.float32) < live, 1.0 / TIMES, 0.0)
     for n in range(COLUMNS // 256):
         right = columns[k, :, pl.ds(pl.multiple_of(part * COLUMNS + n * 256, 256), 256)]
-        for i in range(2):
-            product = jnp.dot(left[i * HALF : (i + 1) * HALF], right, preferred_element_type=jnp.float32)
+        turned = jnp.concatenate([-right[TIMES:], right[:TIMES]], axis=0)
+        for i, other in enumerate((right, turned)):
+            product = jnp.dot(left[...], other, preferred_element_type=jnp.float32)
             out_ref[0, 0, i, :, n * 256 : (n + 1) * 256] = (product * scale).astype(jnp.bfloat16)
 
 
@@ -396,7 +402,7 @@
             pl.BlockSpec(memory_space=pltpu.VMEM),
         ],
         out_specs=pl.BlockSpec((1, 1, 2, HALF, COLUMNS), lambda k, i: (0, k, 0, 0, i)),
-        scratch_shapes=[pltpu.VMEM((TOTAL, 2 * TIMES), jnp.bfloat16)],
+        scratch_shapes=[pltpu.VMEM((HALF, 2 * TIMES), jnp.bfloat16)],
         compiler_params=pltpu.CompilerParams(vmem_limit_bytes=32 * 1024 * 1024),
         name="correlate",
     )(columns, chan_counts.reshape(1, LANES))

time: 51.3 us -> 49.4 us (0.963)
  local copies, waits for them, and re-layouts: 1.05 us -> 0.01 us
  Pallas kernels: 50.2 us -> 49.3 us
    unnamed x8 -> x6, local copies, waits for them, and re-layouts: 1.05 us -> 0.01 us
    pallas_call x1, Pallas kernels: 41.3 us -> 40.7 us  [run_filter_and_turn(): pl.pallas_call(filter_and_turn, out_shape=jax.ShapeDtypeStruct((CAP, 2 *...]
where the time goes in v4:
time: 49.4 us; the launch traced here: 49.3 us
  Pallas kernels  49.3 us (100%)
    pallas_call x1, Pallas kernels, run_filter_and_turn(): pl.pallas_call(filter_and_turn, out_shape=jax.ShapeDtypeStruct((CAP, 2 *...  40.7 us
    pallas_call x1, Pallas kernels, run_correlate(): pl.pallas_call(correlate, grid=(CAP, TOTAL // COLUMNS), out_shape=jax.Sha...  5.1 us
    pallas_call x1, Pallas kernels, run_bring_in(): pl.pallas_call(bring_in, out_shape=jax.ShapeDtypeStruct((FRAMES, TILES, S...  3.47 us

profile of v4, /device:TPU:8, one launch (start us, length us, event | category | flops | bytes accessed | tf_op | source)
XLA Modules:
  0.0 49.3 jit_solution(12288654776449978449)
XLA Ops:
  0.0 0.0 copy-start
  0.0 0.0 copy-start.1
  0.0 0.0 copy-start.2
  0.0 3.5 %bring_in.1 = bf16[63,32,8,2,128]{4,3,2,1,0:T(2,128)(2,1)S(1)} custom-call(bf16[8,63,32,2,128]{4,3,2,1,0:T(2,128)(2,1)} %bitcast.10), custom_call_target="tpu_custom_call" | custom-call | tf_op jit(solution)/shard_map/bring_in/pallas_call | solution.py:121
  3.5 0.0 copy-done
  3.5 0.0 copy-done.1
  3.5 0.0 copy-done.2
  3.5 40.7 %filter_and_turn.1.columns = bf16[3,192,1024]{2,1,0:T(8,128)(2,1)S(1)} custom-call(bf16[63,32,16,128]{3,2,1,0:T(8,128)(2,1)S(1)} %bitcast.6, f32[32,16,128]{2,1,0:T(8,128)S(1)} %copy-done, bf16[16384,512]{1,0:T(8,128)(2,1)} %constant.5.clone.table_ref, s32[1,128]{1,0:T(1,128)S(1)} %bitcast.7, s32[4,128]{1,0:T(4,128)S(1)} %bitcast.9), custom_call_target="tpu_custom_call" | custom-call | tf_op jit(solution)/shard_map/filter_and_turn/pallas_call | solution.py:333
  44.2 5.1 %correlate.1 = bf16[1,3,2,512,1024]{4,3,2,1,0:T(8,128)(2,1)} custom-call(bf16[3,192,1024]{2,1,0:T(8,128)(2,1)S(1)} %filter_and_turn.1.columns, s32[1,128]{1,0:T(1,128)S(1)} %bitcast.8), custom_call_target="tpu_custom_call" | custom-call | tf_op jit(solution)/shard_map/correlate/pallas_call | solution.py:396
Async XLA Ops:
  0.0 3.5 %copy-start = (f32[32,16,128]{2,1,0:T(8,128)S(1)}, f32[32,16,128]{2,1,0:T(8,128)}, u32[]{:S(2)}) copy-start(f32[32,16,128]{2,1,0:T(8,128)} %constant.4.clone.tap_ref) | copy-start | bytes 786436
  0.0 3.5 %copy-start.1 = (s32[128]{0:T(128)S(1)}, s32[128]{0:T(128)}, u32[]{:S(2)}) copy-start(s32[128]{0:T(128)} %param.7) | copy-start | bytes 1540
  0.0 3.5 %copy-start.2 = (s32[512]{0:T(512)S(1)}, s32[512]{0:T(512)}, u32[]{:S(2)}) copy-start(s32[512]{0:T(512)} %param.6) | copy-start | bytes 6148

commit v5 on v4

--- a/solution.py
+++ b/solution.py
@@ -262,12 +262,12 @@
         drain(stage.at[c, pl.ds(0, 15)], recv_z.at[c])
         own_x(c, 0).start()
         own_x(c, 1).start()
-        for j in range(1, 4):
+        for j in (2, 1, 3):
             x_to = lax.rem(x + j, 4)
             remote(
                 stage.at[c, :, x_to * 2 + 1 - y_hi], other.at[c, x], send_x.at[1, c], recv_x.at[1, c], ring_x[j - 1]
             )
-        for j in range(1, 4):
+        for j in (2, 1, 3):
             x_to = lax.rem(x + j, 4)
             remote(
                 stage.at[c, :, x_to * 2 + y_hi], got.at[c, y, x], send_x.at[0, c], recv_x.at[0, c], ring_x[j - 1]
@@ -307,8 +307,8 @@
     bank.finish(sent.at[2])
     go_z(2)
     go_y(0)
+    go_x(1)
     build_places(map_ref, places)
-    go_x(1)
     go_forward(0)
     go_y(1)
     go_x(2)

time: 49.4 us -> 49.1 us (level)
  no operation moved by 1% of the time
where the time goes in v5:
time: 49.1 us; the launch traced here: 49 us
  Pallas kernels  49 us (100%)
    pallas_call x1, Pallas kernels, run_filter_and_turn(): pl.pallas_call(filter_and_turn, out_shape=jax.ShapeDtypeStruct((CAP, 2 *...  40.4 us
    pallas_call x1, Pallas kernels, run_correlate(): pl.pallas_call(correlate, grid=(CAP, TOTAL // COLUMNS), out_shape=jax.Sha...  5.1 us
    pallas_call x1, Pallas kernels, run_bring_in(): pl.pallas_call(bring_in, out_shape=jax.ShapeDtypeStruct((FRAMES, TILES, S...  3.47 us

profile of v5, /device:TPU:8, one launch (start us, length us, event | category | flops | bytes accessed | tf_op | source)
XLA Modules:
  0.0 49.0 jit_solution(4183250773759090567)
XLA Ops:
  0.0 0.0 copy-start
  0.0 0.0 copy-start.1
  0.0 0.0 copy-start.2
  0.0 3.5 %bring_in.1 = bf16[63,32,8,2,128]{4,3,2,1,0:T(2,128)(2,1)S(1)} custom-call(bf16[8,63,32,2,128]{4,3,2,1,0:T(2,128)(2,1)} %bitcast.10), custom_call_target="tpu_custom_call" | custom-call | tf_op jit(solution)/shard_map/bring_in/pallas_call | solution.py:121
  3.5 0.0 copy-done
  3.5 0.0 copy-done.1
  3.5 0.0 copy-done.2
  3.5 40.4 %filter_and_turn.1.columns = bf16[3,192,1024]{2,1,0:T(8,128)(2,1)S(1)} custom-call(bf16[63,32,16,128]{3,2,1,0:T(8,128)(2,1)S(1)} %bitcast.6, f32[32,16,128]{2,1,0:T(8,128)S(1)} %copy-done, bf16[16384,512]{1,0:T(8,128)(2,1)} %constant.5.clone.table_ref, s32[1,128]{1,0:T(1,128)S(1)} %bitcast.7, s32[4,128]{1,0:T(4,128)S(1)} %bitcast.9), custom_call_target="tpu_custom_call" | custom-call | tf_op jit(solution)/shard_map/filter_and_turn/pallas_call | solution.py:333
  43.9 5.1 %correlate.1 = bf16[1,3,2,512,1024]{4,3,2,1,0:T(8,128)(2,1)} custom-call(bf16[3,192,1024]{2,1,0:T(8,128)(2,1)S(1)} %filter_and_turn.1.columns, s32[1,128]{1,0:T(1,128)S(1)} %bitcast.8), custom_call_target="tpu_custom_call" | custom-call | tf_op jit(solution)/shard_map/correlate/pallas_call | solution.py:396
Async XLA Ops:
  0.0 3.5 %copy-start = (f32[32,16,128]{2,1,0:T(8,128)S(1)}, f32[32,16,128]{2,1,0:T(8,128)}, u32[]{:S(2)}) copy-start(f32[32,16,128]{2,1,0:T(8,128)} %constant.4.clone.tap_ref) | copy-start | bytes 786436
  0.0 3.5 %copy-start.1 = (s32[128]{0:T(128)S(1)}, s32[128]{0:T(128)}, u32[]{:S(2)}) copy-start(s32[128]{0:T(128)} %param.7) | copy-start | bytes 1540
  0.0 3.5 %copy-start.2 = (s32[512]{0:T(512)S(1)}, s32[512]{0:T(512)}, u32[]{:S(2)}) copy-start(s32[512]{0:T(512)} %param.6) | copy-start | bytes 6148
